TPU v7x, 768 devices: a whole 4x8x12 slice. The times are simulated.
768 devices in a mesh: group: 24 (over z, core), sub: 32 (over y, x).
Axes of the slice: x: 4, y: 8, z: 12, core: 2. Of those that a mesh axis runs over, the one named last changes fastest.
Arguments:
- load: float32 [8, 12288, 256], P(None, ('group', 'sub'))
- row_scale: float32 [12288, 256], P(('group', 'sub'))
- diag_blocks: bfloat16 [12288, 256, 256], P(('group', 'sub')), may hold values from -0.01184082 to 0.01184082
- off_blocks: bfloat16 [12288, 256, 256], P(('group', 'sub')), may hold values from -0.01184082 to 0.01184082
- off_pattern: int32 [768, 16], P(('group', 'sub')), may hold values from 0 to 15, each once within a row
- partner: int32 [768, 16], P(('group', 'sub')), may hold values from 0 to 31, as said below
- corner_coupling: bfloat16 [6144, 4096], P(('group', 'sub')), may hold values from -0.375 to 0.375
- corner_index: int32 [24, 256], P('group'), may hold values from 0 to 127
- coarse_inverse: float32 [3072, 128], P('group'), as said below
Outputs:
- multipliers: float32 [8, 12288, 256], P(None, ('group', 'sub'))
- residual: float32 [8, 12288, 256], P(None, ('group', 'sub'))
Inputs may be any that keep to these rules, and one draw needn't show every extreme that they name: partner[s, i] is t XOR m for the subdomain s = 32 * grp + t, with m nonzero and depending only on grp and i; so block i of s and block i of its partner share one multiplier. No subdomain shares more than 1 block with one other subdomain, and some share exactly 1. `coarse_inverse`: each cluster's block is symmetric and positive definite.
All inputs are finite; a program needn't handle non-finite values.
Results may differ from a plain program's by a relative error of at most 0.012.
The roundings to bfloat16 on the way count: a program that leaves them out, or rounds other values in their place, can miss the bound.
Values sent between devices are 32-bit elements; how exact they have to be, the bound alone decides.
A program may use at most 32 MiB of HBM per device.

v0:
```python
import jax
import jax.numpy as jnp
from jax import lax
from jax.sharding import PartitionSpec as P

ITERS = 4


HIGH = lax.Precision.HIGHEST


def on_device(
    load,
    row_scale,
    diag_blocks,
    off_blocks,
    off_pattern,
    partner,
    corner_coupling,
    corner_index,
    coarse_inverse,
):
    blocks = diag_blocks.shape[0]
    width = diag_blocks.shape[1]
    columns = load.shape[0]
    corners = corner_coupling.shape[0]
    coarse = coarse_inverse.shape[1]
    peers = lax.axis_size("sub")
    myself = lax.axis_index("sub")
    sigma = off_pattern[0]
    mates = partner[0]
    block_ids = jnp.arange(blocks, dtype=jnp.int32)
    select = sigma[:, None] == block_ids[None, :]
    select_half = select.astype(jnp.bfloat16)
    select_full = select.astype(jnp.float32)
    coarse_ids = jnp.arange(coarse, dtype=jnp.int32)
    own_index = lax.dynamic_slice_in_dim(corner_index[0], myself * corners, corners, 0)
    own_onehot = (own_index[:, None] == coarse_ids[None, :]).astype(jnp.float32)

    def jump(field):
        capacity = (blocks + peers - 2) // (peers - 1)
        same = mates[:, None] == mates[None, :]
        lower = block_ids[:, None] < block_ids[None, :]
        rank = jnp.sum((same & lower).astype(jnp.int32), axis=0)
        peer_ids = jnp.arange(peers, dtype=jnp.int32)
        slot_ids = jnp.arange(capacity, dtype=jnp.int32)
        slots = (
            (mates[None, None, :] == peer_ids[:, None, None])
            & (rank[None, None, :] == slot_ids[None, :, None])
        ).astype(jnp.float32)
        outgoing = jnp.einsum("jcb,nbk->jcnk", slots, field, precision=HIGH)
        incoming = lax.all_to_all(outgoing, "sub", split_axis=0, concat_axis=0, tiled=True)
        other = jnp.einsum("jcb,jcnk->nbk", slots, incoming, precision=HIGH)
        return field - other

    def column(first, second):
        return jnp.sum(first * second, axis=(1, 2))

    def total(value):
        inner = lax.psum(value, "sub")
        return lax.psum(inner, "group")

    def widen(value):
        return value[:, None, None]

    residual = jump(load)
    multipliers = jnp.zeros_like(residual)
    direction = residual
    norm_now = total(column(residual, residual))
    for step in range(ITERS):
        scaled = (row_scale[None] * direction).astype(jnp.bfloat16)
        moved = jnp.einsum(
            "ij,njl->nil", select_half, scaled, preferred_element_type=jnp.float32
        ).astype(jnp.bfloat16)
        coupled = jnp.einsum(
            "ikl,nil->nik", diag_blocks, scaled, preferred_element_type=jnp.float32
        )
        coupled = coupled + jnp.einsum(
            "ilk,nil->nik", diag_blocks, scaled, preferred_element_type=jnp.float32
        )
        coupled = coupled + jnp.einsum(
            "ikl,nil->nik", off_blocks, moved, preferred_element_type=jnp.float32
        )
        back = jnp.einsum("ilk,nil->nik", off_blocks, scaled, preferred_element_type=jnp.float32)
        coupled = coupled + jnp.einsum("ij,nik->njk", select_full, back, precision=HIGH)
        flat = scaled.reshape(columns, blocks * width)
        partial_terms = lax.dot_general(
            flat, corner_coupling, (((1,), (1,)), ((), ())), preferred_element_type=jnp.float32
        )
        spread = jnp.dot(partial_terms, own_onehot, precision=HIGH)
        gathered = lax.psum(spread, "sub")
        solved = jnp.dot(gathered, coarse_inverse.T, precision=HIGH)
        local = jnp.dot(solved, own_onehot.T, precision=HIGH).astype(jnp.bfloat16)
        lifted = jnp.dot(local, corner_coupling, preferred_element_type=jnp.float32).reshape(
            columns, blocks, width
        )
        product = jump(row_scale[None] * (scaled.astype(jnp.float32) + coupled + lifted))
        alpha = norm_now / total(column(direction, product))
        multipliers = multipliers + widen(alpha) * direction
        residual = residual - widen(alpha) * product
        norm_next = total(column(residual, residual))
        direction = residual + widen(norm_next / norm_now) * direction
        norm_now = norm_next
    return (multipliers, residual)


def solution(mesh):
    return jax.shard_map(
        on_device,
        mesh=mesh,
        in_specs=(
            P(None, ("group", "sub"), None),
            P(("group", "sub"), None),
            P(("group", "sub"), None, None),
            P(("group", "sub"), None, None),
            P(("group", "sub"), None),
            P(("group", "sub"), None),
            P(("group", "sub"), None),
            P("group", None),
            P("group", None),
        ),
        out_specs=(P(None, ("group", "sub"), None), P(None, ("group", "sub"), None)),
        check_vma=False,
    )
```

profile of v0, /device:TPU:1, one launch (start us, length us, event | category | flops | bytes accessed | tf_op | source)
XLA Modules:
  0.0 1154.1 jit_solution(7484176229010402699)
XLA Ops:
  0.6 0.9 convert_reduce_fusion
  1.6 1.3 convolution_bitcast_fusion.4
  2.9 0.8 copy.61
  3.7 10.5 all-to-all-start
  14.2 0.7 dynamic-slice_bitcast_fusion
  14.9 9.8 all-to-all-done
  24.7 1.2 multiply_convert_fusion.3
  26.0 0.4 fusion.63
  26.4 0.6 fusion.65
  27.4 56.4 %psum.142 = f32[8,128]{1,0:T(8,128)S(1)} all-reduce(f32[8,128]{1,0:T(8,128)S(1)} %fusion.89), channel_id=1, replica_groups=mesh['group'=24,'sub'=32] {'sub'}, use_global_device_ids=true, to_apply=%region_4.0 | all-reduce | flops 1024 | bytes 8192 | tf_op jit(solution)/shard_map/psum | solution.py:91
  84.2 0.3 fusion.21
  84.5 2.0 convolution_bitcast_fusion.16
  86.5 0.6 fusion.45
  87.3 0.3 fusion.7
  87.6 0.4 convolution_bitcast_fusion.3
  88.1 15.3 %all_to_all.25 = f32[32,1,8,256]{3,2,1,0:T(8,128)S(1)} all-to-all(f32[32,1,8,256]{3,2,1,0:T(8,128)S(1)} %copy.72), channel_id=1, replica_groups=mesh['group'=24,'sub'=32] {'sub'}, dimensions={0} | all-to-all | bytes 524288 | tf_op jit(solution)/shard_map/all_to_all | solution.py:52
  103.4 0.4 multiply_reduce_fusion.6
  103.9 56.5 %all-reduce = (f32[8]{0:T(128)S(1)}, f32[8]{0:T(128)S(1)}) all-reduce(f32[8]{0:T(128)S(1)} %get-tuple-element.3, f32[8]{0:T(128)S(1)} %get-tuple-element.2), channel_id=1, replica_groups=mesh['group'=24,'sub'=32] {'sub'}, use_global_device_ids=true, to_apply=%region_2.0 | all-reduce | flops 16 | bytes 128 | tf_op jit(solution)/shard_map/psum | solution.py:60
  160.4 77.2 %all-reduce.1 = (f32[8]{0:T(128)S(1)}, f32[8]{0:T(128)S(1)}) all-reduce(f32[8]{0:T(128)S(1)} %get-tuple-element.4, f32[8]{0:T(128)S(1)} %get-tuple-element.5), channel_id=1, replica_groups=mesh['group'=24,'sub'=32] {'group'}, use_global_device_ids=true, to_apply=%region_3.0 | all-reduce | flops 16 | bytes 128 | tf_op jit(solution)/shard_map/psum | solution.py:61
  237.6 0.2 multiply_reduce_fusion.5
  237.8 57.0 %psum.145 = f32[8]{0:T(128)S(1)} all-reduce(f32[8]{0:T(128)S(1)} %multiply_reduce_fusion.5), channel_id=1, replica_groups=mesh['group'=24,'sub'=32] {'sub'}, use_global_device_ids=true, to_apply=%region_9.0 | all-reduce | flops 8 | bytes 64 | tf_op jit(solution)/shard_map/psum | solution.py:60
  294.8 48.1 %psum.146 = f32[8]{0:T(128)S(1)} all-reduce(f32[8]{0:T(128)S(1)} %psum.145), channel_id=1, replica_groups=mesh['group'=24,'sub'=32] {'group'}, use_global_device_ids=true, to_apply=%region_10.0 | all-reduce | flops 8 | bytes 64 | tf_op jit(solution)/shard_map/psum | solution.py:61
  343.2 0.4 fusion.58
  343.6 0.9 copy-done.2
  344.5 0.4 convolution_bitcast_fusion.13
  344.9 0.6 fusion.60
  345.9 56.3 %psum.147 = f32[8,128]{1,0:T(8,128)S(1)} all-reduce(f32[8,128]{1,0:T(8,128)S(1)} %fusion.88), channel_id=1, replica_groups=mesh['group'=24,'sub'=32] {'sub'}, use_global_device_ids=true, to_apply=%region_11.0 | all-reduce | flops 1024 | bytes 8192 | tf_op jit(solution)/shard_map/psum | solution.py:91
  402.6 2.3 fusion.43
  405.0 0.3 fusion.11
  405.3 0.4 convolution_bitcast_fusion.2
  405.9 15.1 %all_to_all.26 = f32[32,1,8,256]{3,2,1,0:T(8,128)S(1)} all-to-all(f32[32,1,8,256]{3,2,1,0:T(8,128)S(1)} %copy.83), channel_id=1, replica_groups=mesh['group'=24,'sub'=32] {'sub'}, dimensions={0} | all-to-all | bytes 524288 | tf_op jit(solution)/shard_map/all_to_all | solution.py:52
  421.0 0.4 multiply_reduce_fusion.4
  421.4 57.1 %psum.148 = f32[8]{0:T(128)S(1)} all-reduce(f32[8]{0:T(128)S(1)} %get-tuple-element.21), channel_id=1, replica_groups=mesh['group'=24,'sub'=32] {'sub'}, use_global_device_ids=true, to_apply=%region_13.0 | all-reduce | flops 8 | bytes 64 | tf_op jit(solution)/shard_map/psum | solution.py:60
  478.5 64.0 %psum.149 = f32[8]{0:T(128)S(1)} all-reduce(f32[8]{0:T(128)S(1)} %psum.148), channel_id=1, replica_groups=mesh['group'=24,'sub'=32] {'group'}, use_global_device_ids=true, to_apply=%region_14.0 | all-reduce | flops 8 | bytes 64 | tf_op jit(solution)/shard_map/psum | solution.py:61
  542.7 57.2 %psum.150 = f32[8]{0:T(128)S(1)} all-reduce(f32[8]{0:T(128)S(1)} %get-tuple-element.12), channel_id=1, replica_groups=mesh['group'=24,'sub'=32] {'sub'}, use_global_device_ids=true, to_apply=%region_16.0 | all-reduce | flops 8 | bytes 64 | tf_op jit(solution)/shard_map/psum | solution.py:60
  599.8 48.4 %psum.151 = f32[8]{0:T(128)S(1)} all-reduce(f32[8]{0:T(128)S(1)} %psum.150), channel_id=1, replica_groups=mesh['group'=24,'sub'=32] {'group'}, use_global_device_ids=true, to_apply=%region_17.0 | all-reduce | flops 8 | bytes 64 | tf_op jit(solution)/shard_map/psum | solution.py:61
  648.6 0.4 fusion.53
  649.0 0.9 copy-done.3
  649.9 0.4 convolution_bitcast_fusion.10
  650.3 0.6 fusion.55
  651.3 56.3 %psum.152 = f32[8,128]{1,0:T(8,128)S(1)} all-reduce(f32[8,128]{1,0:T(8,128)S(1)} %fusion.87), channel_id=1, replica_groups=mesh['group'=24,'sub'=32] {'sub'}, use_global_device_ids=true, to_apply=%region_18.0 | all-reduce | flops 1024 | bytes 8192 | tf_op jit(solution)/shard_map/psum | solution.py:91
  707.9 2.3 fusion.41
  710.4 0.3 fusion.15
  710.7 0.4 convolution_bitcast_fusion.1
  711.2 15.1 %all_to_all.27 = f32[32,1,8,256]{3,2,1,0:T(8,128)S(1)} all-to-all(f32[32,1,8,256]{3,2,1,0:T(8,128)S(1)} %copy.94), channel_id=1, replica_groups=mesh['group'=24,'sub'=32] {'sub'}, dimensions={0} | all-to-all | bytes 524288 | tf_op jit(solution)/shard_map/all_to_all | solution.py:52
  726.3 0.4 multiply_reduce_fusion.2
  726.7 57.1 %psum.153 = f32[8]{0:T(128)S(1)} all-reduce(f32[8]{0:T(128)S(1)} %get-tuple-element.23), channel_id=1, replica_groups=mesh['group'=24,'sub'=32] {'sub'}, use_global_device_ids=true, to_apply=%region_20.0 | all-reduce | flops 8 | bytes 64 | tf_op jit(solution)/shard_map/psum | solution.py:60
  783.8 64.0 %psum.154 = f32[8]{0:T(128)S(1)} all-reduce(f32[8]{0:T(128)S(1)} %psum.153), channel_id=1, replica_groups=mesh['group'=24,'sub'=32] {'group'}, use_global_device_ids=true, to_apply=%region_21.0 | all-reduce | flops 8 | bytes 64 | tf_op jit(solution)/shard_map/psum | solution.py:61
  847.8 0.2 multiply_reduce_fusion.1
  848.0 57.2 %psum.155 = f32[8]{0:T(128)S(1)} all-reduce(f32[8]{0:T(128)S(1)} %get-tuple-element.8), channel_id=1, replica_groups=mesh['group'=24,'sub'=32] {'sub'}, use_global_device_ids=true, to_apply=%region_23.0 | all-reduce | flops 8 | bytes 64 | tf_op jit(solution)/shard_map/psum | solution.py:60
  905.2 48.6 %psum.156 = f32[8]{0:T(128)S(1)} all-reduce(f32[8]{0:T(128)S(1)} %psum.155), channel_id=1, replica_groups=mesh['group'=24,'sub'=32] {'group'}, use_global_device_ids=true, to_apply=%region_24.0 | all-reduce | flops 8 | bytes 64 | tf_op jit(solution)/shard_map/psum | solution.py:61
  954.1 0.4 fusion.48
  954.5 0.9 copy-done.4
  955.4 0.4 convolution_bitcast_fusion.7
  955.8 0.6 fusion.50
  956.8 56.3 %psum.157 = f32[8,128]{1,0:T(8,128)S(1)} all-reduce(f32[8,128]{1,0:T(8,128)S(1)} %fusion.86), channel_id=1, replica_groups=mesh['group'=24,'sub'=32] {'sub'}, use_global_device_ids=true, to_apply=%region_25.0 | all-reduce | flops 1024 | bytes 8192 | tf_op jit(solution)/shard_map/psum | solution.py:91
  1013.5 2.3 fusion.39
  1015.9 0.3 fusion.19
  1016.2 0.4 convolution_bitcast_fusion
  1016.7 15.1 %all_to_all.28 = f32[32,1,8,256]{3,2,1,0:T(8,128)S(1)} all-to-all(f32[32,1,8,256]{3,2,1,0:T(8,128)S(1)} %copy.105), channel_id=1, replica_groups=mesh['group'=24,'sub'=32] {'sub'}, dimensions={0} | all-to-all | bytes 524288 | tf_op jit(solution)/shard_map/all_to_all | solution.py:52
  1031.8 0.4 multiply_reduce_fusion
  1032.3 57.1 %psum.158 = f32[8]{0:T(128)S(1)} all-reduce(f32[8]{0:T(128)S(1)} %get-tuple-element.25), channel_id=1, replica_groups=mesh['group'=24,'sub'=32] {'sub'}, use_global_device_ids=true, to_apply=%region_27.0 | all-reduce | flops 8 | bytes 64 | tf_op jit(solution)/shard_map/psum | solution.py:60
  1089.3 64.0 %psum.159 = f32[8]{0:T(128)S(1)} all-reduce(f32[8]{0:T(128)S(1)} %psum.158), channel_id=1, replica_groups=mesh['group'=24,'sub'=32] {'group'}, use_global_device_ids=true, to_apply=%region_28.0 | all-reduce | flops 8 | bytes 64 | tf_op jit(solution)/shard_map/psum | solution.py:61
  1153.3 0.8 multiply_subtract_fusion
  (60 shorter events, 5.4 us)
Async XLA Ops:
  0.6 25.3 %copy-start = (bf16[16,256,256]{2,1,0:T(8,128)(2,1)S(1)}, bf16[16,256,256]{2,1,0:T(8,128)(2,1)}, u32[]{:S(2)}) copy-start(bf16[16,256,256]{2,1,0:T(8,128)(2,1)} %param.11) | copy-start | bytes 6291460
  3.7 21.0 %all-to-all-start = ((f32[32,1,8,256]{3,2,1,0:T(8,128)}), f32[32,1,8,256]{3,2,1,0:T(8,128)S(1)}, u32[]{:S(2)}, u32[]{:S(2)}) async-start(f32[32,1,8,256]{3,2,1,0:T(8,128)} %copy.61), calls=%async_computation | async-start | bytes 524288 | tf_op jit(solution)/shard_map/all_to_all | solution.py:52
  26.0 1.1 copy-start.5
  26.0 57.9 %copy-start.6 = (f32[128,128]{1,0:T(8,128)S(1)}, f32[128,128]{1,0:T(8,128)}, u32[]{:S(2)}) copy-start(f32[128,128]{1,0:T(8,128)} %param.17) | copy-start | bytes 196612
  26.0 58.2 %copy-start.9 = (s32[1,16]{1,0:T(1,128)S(1)}, s32[1,16]{1,0:T(1,128)}, u32[]{:S(2)}) copy-start(s32[1,16]{1,0:T(1,128)} %param.13) | copy-start | bytes 196
  83.8 2.6 copy-start.1
  84.5 2.8 copy-start.7
  86.5 1.1 copy-start.8
  342.9 1.6 copy-start.2
  648.3 1.6 copy-start.3
  953.8 1.6 copy-start.4
where the time goes:
time: 1160 us; the launch traced here: 1150 us
  blocking collectives  1100 us (95%)
  matrix products  25.9 us (2%)
    psum x7, blocking collectives, total(): return lax.psum(inner, 'group')  414 us
    psum x7, blocking collectives, total(): inner = lax.psum(value, 'sub')  399 us
    psum x4, blocking collectives, on_device(): gathered = lax.psum(spread, 'sub')  225 us
    all_to_all x4, blocking collectives, jump(): lax.all_to_all(outgoing, 'sub', split_axis=0, concat_axis=0, tiled=True)  60.6 us
  transfers between devices with their start and end apart: 1, of which 1 were waited for; matrix products, arithmetic and copies ran while one was open for 0% of the time, Pallas kernels for 0%

commit v1 on v0

v1 whole, which is shorter than its diff:
```python
import jax
import jax.numpy as jnp
from jax import lax
from jax.experimental import pallas as pl
from jax.experimental.pallas import tpu as pltpu
from jax.sharding import PartitionSpec as P

ITERS = 4
MESH = pl.DeviceIdType.MESH
F32 = jnp.float32
BF16 = jnp.bfloat16


def dot(a, b):
    return jnp.dot(a, b, preferred_element_type=F32)


def split(x):
    high = x.astype(BF16)
    return high, (x - high.astype(F32)).astype(BF16)


def iota(shape, axis):
    return lax.broadcasted_iota(jnp.int32, shape, axis)


def kernel(
    load_hbm,
    scale_hbm,
    diag_hbm,
    off_hbm,
    pattern_hbm,
    partner_hbm,
    coupling_hbm,
    index_hbm,
    inverse_hbm,
    mult_ref,
    res_ref,
    load_ref,
    scale_ref,
    diag,
    off,
    pattern_ref,
    partner_ref,
    coupling_ref,
    index_ref,
    inverse_ref,
    basis,
    image,
    field,
    stacked,
    back,
    coarse_rows,
    coarse_wide,
    lift_high,
    lift_low,
    lift,
    onehot,
    pick,
    local,
    info,
    norms,
    ritzes,
    direction,
    residual,
    multipliers,
    squares,
    landing,
    slot_block,
    block_slot,
    inverse_pattern,
    row_send,
    dot_send,
    group_send,
    send,
    recv,
    row_recv,
    dot_recv,
    group_recv,
    local_sem,
    send_sem,
    row_send_sem,
    dot_send_sem,
    group_send_sem,
    recv_sem,
    row_sem,
    dot_sem,
    group_sem,
):
    groups = lax.axis_size("group")
    peers = lax.axis_size("sub")
    group = lax.axis_index("group")
    me = lax.axis_index("sub")
    blocks = 16
    corners = 8

    pairs = (
        (partner_hbm, partner_ref),
        (pattern_hbm, pattern_ref),
        (load_hbm, load_ref),
        (scale_hbm, scale_ref),
        (coupling_hbm, coupling_ref),
        (index_hbm, index_ref),
        (inverse_hbm, inverse_ref),
        (diag_hbm, diag),
        (off_hbm, off),
    )
    copies = [pltpu.make_async_copy(a, b, local_sem.at[k]) for k, (a, b) in enumerate(pairs)]
    for copy in copies:
        copy.start()

    barrier = pltpu.get_barrier_semaphore()

    @pl.loop(1, peers)
    def _(o):
        pl.semaphore_signal(
            barrier, inc=1, device_id={"sub": lax.rem(me + o, peers)}, device_id_type=MESH
        )

    @pl.loop(1, groups)
    def _(o):
        pl.semaphore_signal(
            barrier, inc=1, device_id={"group": lax.rem(group + o, groups)}, device_id_type=MESH
        )

    def all_offsets(body):
        @pl.loop(0, peers - 4)
        def _(s):
            q = s // 4
            far = 4 + ((q + 1) // 2) * (1 - 2 * (q % 2))
            body(4 * far + s % 4)

        @pl.loop(1, 4)
        def _(o):
            body(o)

    def swap_field(source, number):
        def one(o):
            send[number, o] = source[slot_block[o]]
            pltpu.make_async_remote_copy(
                src_ref=send.at[number, o],
                dst_ref=recv.at[number, o],
                send_sem=send_sem.at[number],
                recv_sem=recv_sem.at[number],
                device_id={"sub": lax.rem(me + o, peers)},
                device_id_type=MESH,
            ).start()

        all_offsets(one)

    def wait_field(number):
        rest = pl.ds(1, peers - 1)
        ref = recv.at[number, rest]
        pltpu.make_async_copy(ref, ref, recv_sem.at[number]).wait()
        ref = send.at[number, rest]
        pltpu.make_async_copy(ref, ref, send_sem.at[number]).wait()
        for o in range(1, 32):
            landing[o] = recv[number, o]

    def swap_row(row, source, target, step, out_sem, in_sem):
        source[step] = row
        target[step, 0] = row

        def one(o):
            pltpu.make_async_remote_copy(
                src_ref=source.at[step],
                dst_ref=target.at[step, o],
                send_sem=out_sem.at[step],
                recv_sem=in_sem.at[step],
                device_id={"sub": lax.rem(me + o, peers)},
                device_id_type=MESH,
            ).start()

        all_offsets(one)

    def wait_row(target, step, out_sem, in_sem):
        ref = target.at[step, pl.ds(1, peers - 1)]
        pltpu.make_async_copy(ref, ref, in_sem.at[step]).wait()
        pltpu.make_async_copy(ref, ref, out_sem.at[step]).wait()

    lane = iota((8, 128), 1)
    sub = iota((8, 128), 0)

    def to_row(columns):
        total = jnp.zeros((8, 128), F32)
        for k, c in enumerate(columns):
            total = jnp.where(lane // 8 == k, c, total)
        return jnp.sum(jnp.where(lane % 8 == sub, total, 0.0), axis=0, keepdims=True)

    def to_column(row):
        return jnp.sum(jnp.where(lane == sub, row, 0.0), axis=1, keepdims=True)

    def over(top, bottom, other):
        return jnp.where(bottom > 0.0, top / jnp.where(bottom > 0.0, bottom, 1.0), other)

    def wide(row):
        return jnp.broadcast_to(row, (8, 128))

    def swap_group(row, number):
        group_send[number] = row
        group_recv[number, 0] = row

        @pl.loop(1, groups)
        def _(o):
            pltpu.make_async_remote_copy(
                src_ref=group_send.at[number],
                dst_ref=group_recv.at[number, o],
                send_sem=group_send_sem.at[number],
                recv_sem=group_sem.at[number],
                device_id={"group": lax.rem(group + o, groups)},
                device_id_type=MESH,
            ).start()

    def wait_group(number):
        ref = group_recv.at[number, pl.ds(1, groups - 1)]
        pltpu.make_async_copy(ref, ref, group_sem.at[number]).wait()
        pltpu.make_async_copy(ref, ref, group_send_sem.at[number]).wait()
        return group_recv[number].reshape(groups, 128)

    def positive(ritz):
        return jnp.where(ritz == 0.0, 1.0, jnp.abs(ritz))

    def advance():
        d = [direction[j] for j in range(ITERS + 1)]
        weight = [norms[j] for j in range(ITERS)]
        a = [ritzes[j] for j in range(ITERS)]
        product = [a[j] * d[j] for j in range(ITERS)] + [jnp.zeros_like(d[0])]
        for j in range(ITERS):
            growth = positive(a[j])
            product[j + 1] = product[j + 1] + growth * d[j]
            if j < ITERS - 1:
                product[j] = product[j] + over(weight[j + 1] * growth, weight[j], 0.0) * d[j + 1]

        def total(left, right):
            value = weight[0] * left[0] * right[0]
            for j in range(1, ITERS):
                value = value + weight[j] * left[j] * right[j]
            return jnp.sum(value, axis=0, keepdims=True)

        now = squares[0:1]
        alpha = now / total(d, product)
        r = [residual[j] - alpha * product[j] for j in range(ITERS + 1)]
        after = total(r, r)
        ratio = after / now
        for j in range(ITERS + 1):
            multipliers[j] = multipliers[j] + alpha * d[j]
            residual[j] = r[j]
            direction[j] = r[j] + ratio * d[j]
        squares[...] = wide(after)

    def own(value):
        return to_column(value[0:1])

    for copy in copies[:2]:
        copy.wait()

    @pl.loop(1, peers)
    def _(o):
        peer = lax.rem(me + o, peers)
        found = jnp.int32(0)
        for i in range(blocks):
            found = jnp.where(partner_ref[0, i] == peer, jnp.int32(i), found)
        slot_block[o] = found

    @pl.loop(0, blocks)
    def _(i):
        found = jnp.int32(0)
        for j in range(blocks):
            found = jnp.where(pattern_ref[0, j] == i, jnp.int32(j), found)
        inverse_pattern[i] = found
        block_slot[i] = lax.rem(me - partner_ref[0, i] + peers, peers)

    for copy in copies[2:5]:
        copy.wait()
    for i in range(blocks):
        field[i] = load_ref[:, i, :]
        scale = scale_ref[i : i + 1, :]
        coarse_rows[i] = coupling_ref[:, 256 * i : 256 * (i + 1)].astype(F32) * scale

    pl.semaphore_wait(barrier, peers - 1 + groups - 1)
    swap_field(field, 0)
    swap_field(coarse_rows, 1)

    for j in range(corners):
        for i in range(blocks):
            row = coupling_ref[:, 256 * i : 256 * (i + 1)].astype(F32)[j : j + 1]
            coarse_wide[j, i] = jnp.broadcast_to(row, (8, 256))
    for copy in copies[5:7]:
        copy.wait()
    natural = (index_ref[...] == iota((128, 256), 0)).astype(BF16)
    p = iota((256, 256), 0)
    q = iota((256, 256), 1)
    order = ((p // 8 == (me - q % 32 + 32) % 32) & (p % 8 == q // 32)).astype(F32).astype(BF16)
    onehot[...] = dot(natural, order).astype(BF16)
    mate = iota((1, 256), 1)
    owner = jnp.zeros((1, 256), jnp.int32) + me
    for i in range(blocks):
        owner = jnp.where((mate // 16 == i) & (mate % 16 >= 8), partner_ref[0, i], owner)
    sign = jnp.where(q % 16 >= 8, -1.0, 1.0)
    choose = jnp.where((p // 8 == owner) & (p % 8 == q % 8), sign, 0.0).astype(BF16)
    pick[...] = dot(natural, choose).astype(BF16)
    for ref in (local, norms, ritzes, direction, residual, multipliers):
        ref[...] = jnp.zeros_like(ref)
    direction[0] = jnp.ones_like(direction[0])
    residual[0] = jnp.ones_like(residual[0])
    for copy in copies[7:]:
        copy.wait()

    @pl.loop(0, blocks)
    def _(i):
        half = diag[i].astype(F32)
        diag[i] = (half + half.T).astype(BF16)

    wait_field(0)
    for i in range(blocks):
        basis[0, i] = field[i] - landing[block_slot[i]]

    @pl.loop(0, ITERS)
    def _(step):
        before = jnp.maximum(step - 1, 0)
        parts = [jnp.zeros((8, 256), F32) for _ in range(corners + 1)]
        for i in range(blocks):
            v = basis[step, i]
            scaled = scale_ref[i : i + 1, :] * v
            high = scaled.astype(BF16).astype(F32)
            scaled = jnp.where(step == 0, high, scaled)
            field[i] = scaled
            stacked[i] = jnp.concatenate([high, scaled - high], axis=0).astype(BF16)
            for j in range(corners):
                parts[j] = parts[j] + scaled * coarse_wide[j, i]
            parts[corners] = parts[corners] + v * v
        row = to_row([jnp.sum(part, axis=1, keepdims=True) for part in parts])
        swap_row(row, row_send, row_recv, step, row_send_sem, row_sem)

        for i in range(blocks):
            x = stacked[i]
            behind = dot(x, off[i])
            back[i] = behind[:8] + behind[8:]
            ahead = dot(x, diag[i]) + lax.dot_general(
                stacked[pattern_ref[0, i]],
                off[i],
                (((1,), (1,)), ((), ())),
                preferred_element_type=F32,
            )
            image[i] = ahead[:8] + ahead[8:]
        product = jnp.zeros((8, 256), F32)
        for i in range(blocks):
            scale = scale_ref[i : i + 1, :]
            scaled = field[i]
            total = scaled + image[i] + back[inverse_pattern[i]]
            product = product + scale * basis[step, i] * total
            image[i] = scale * total
        row = to_row([jnp.sum(product, axis=1, keepdims=True)])
        swap_row(row, dot_send, dot_recv, step, dot_send_sem, dot_sem)
        swap_field(image, step + 2)

        @pl.when(step == 0)
        def _():
            wait_field(1)
            for i in range(blocks):
                rows = jnp.concatenate([coarse_rows[i], landing[block_slot[i]]], axis=0)
                high, low = split(rows)
                lift_high[16 * i : 16 * (i + 1), :] = high
                lift_low[16 * i : 16 * (i + 1), :] = low

        wait_row(row_recv, step, row_send_sem, row_sem)
        rows = row_recv[step].reshape(peers, 128)
        norm = pltpu.roll(wide(jnp.sum(rows, axis=0, keepdims=True)), 64, 1)
        info[step] = norm

        @pl.when(step > 0)
        def _():
            kinds = (info[before], pltpu.roll(norm, 8, 1), pltpu.roll(info[4 + before], 16, 1))
            row = jnp.zeros((8, 128), F32)
            for k, value in enumerate(kinds):
                row = jnp.where(lane // 8 == k, value, row)
            swap_group(row[:1], before)

        high, low = split(
            jnp.concatenate(
                [rows] + [pltpu.roll(rows, 128 - 8 * j, 1) for j in range(1, corners)], axis=0
            )
        )
        gathered = dot(onehot[...], high) + dot(onehot[...], low)
        high, low = split(gathered)
        inverse_high, inverse_low = split(inverse_ref[...])
        solved = dot(inverse_high, high) + (dot(inverse_high, low) + dot(inverse_low, high))
        energy = jnp.sum(gathered * solved, axis=0, keepdims=True)
        high, low = split(solved.T[:8])
        both = jnp.concatenate([high.astype(F32), low.astype(F32)], axis=0).astype(BF16)
        both = dot(both, pick[...])
        local[step] = both[:8] + both[8:]

        wait_row(dot_recv, step, dot_send_sem, dot_sem)
        rows = dot_recv[step].reshape(peers, 128)
        ritz = over(2.0 * wide(jnp.sum(rows, axis=0, keepdims=True) + energy), norm, 0.0)
        old = over(norm * positive(info[4 + before]), info[before], 0.0)
        old = jnp.where(step > 0, old, 0.0)
        info[4 + step] = ritz

        @pl.when(step == ITERS - 1)
        def _():
            swap_group(ritz[:1], ITERS - 1)

        @pl.when(step > 0)
        def _():
            rows = wait_group(before)

            @pl.when(step == 1)
            def _():
                norms[0] = rows
                squares[...] = wide(jnp.sum(rows, axis=0, keepdims=True))

            norms[step] = pltpu.roll(rows, 120, 1)
            ritzes[before] = pltpu.roll(rows, 112, 1)
            advance()

        exact = jnp.zeros((8, 256), F32)
        for j in range(ITERS):
            exact = exact + own(direction[j]) * local[j]
        share = own(direction[step])
        slip = exact.astype(BF16).astype(F32) - exact
        slip = jnp.where(share == 0.0, 0.0, slip / jnp.where(share == 0.0, 1.0, share))
        value = local[step] + slip
        spread = jnp.concatenate(
            [jnp.where(iota((8, 256), 1) // 16 == i, value, 0.0) for i in range(blocks)], axis=0
        )
        high, low = split(spread)
        lift[...] = dot(high, lift_high[...]) + (dot(low, lift_high[...]) + dot(high, lift_low[...]))

        shrink = to_column(1.0 / positive(ritz))
        ritz = to_column(ritz)
        old = to_column(old)
        wait_field(step + 2)
        for i in range(blocks):
            jumped = image[i] - landing[block_slot[i]] + lift[8 * i : 8 * (i + 1), :]
            basis[step + 1, i] = (jumped - ritz * basis[step, i] - old * basis[before, i]) * shrink

    ritzes[ITERS - 1] = wait_group(ITERS - 1)
    advance()
    weights = [own(multipliers[j]) for j in range(ITERS)]
    shares = [own(residual[j]) for j in range(ITERS + 1)]
    for i in range(blocks):
        vectors = [basis[j, i] for j in range(ITERS + 1)]
        value = weights[0] * vectors[0]
        for j in range(1, ITERS):
            value = value + weights[j] * vectors[j]
        mult_ref[i] = value
        value = shares[0] * vectors[0]
        for j in range(1, ITERS + 1):
            value = value + shares[j] * vectors[j]
        res_ref[i] = value


def on_device(
    load,
    row_scale,
    diag_blocks,
    off_blocks,
    off_pattern,
    partner,
    corner_coupling,
    corner_index,
    coarse_inverse,
):
    groups = lax.axis_size("group")
    peers = lax.axis_size("sub")
    vmem = pl.BlockSpec(memory_space=pltpu.VMEM)
    dma = pltpu.SemaphoreType.DMA
    field = jax.ShapeDtypeStruct((16, 8, 256), F32)
    multipliers, residual = pl.pallas_call(
        kernel,
        out_shape=(field, field),
        in_specs=[pl.BlockSpec(memory_space=pl.ANY)] * 9,
        out_specs=(vmem, vmem),
        scratch_shapes=[
            pltpu.VMEM(load.shape, F32),
            pltpu.VMEM(row_scale.shape, F32),
            pltpu.VMEM(diag_blocks.shape, BF16),
            pltpu.VMEM(off_blocks.shape, BF16),
            pltpu.SMEM(off_pattern.shape, jnp.int32),
            pltpu.SMEM(partner.shape, jnp.int32),
            pltpu.VMEM(corner_coupling.shape, BF16),
            pltpu.VMEM(corner_index.shape, jnp.int32),
            pltpu.VMEM(coarse_inverse.shape, F32),
            pltpu.VMEM((ITERS + 1, 16, 8, 256), F32),
            pltpu.VMEM((16, 8, 256), F32),
            pltpu.VMEM((16, 8, 256), F32),
            pltpu.VMEM((16, 16, 256), BF16),
            pltpu.VMEM((16, 8, 256), F32),
            pltpu.VMEM((16, 8, 256), F32),
            pltpu.VMEM((8, 16, 8, 256), F32),
            pltpu.VMEM((256, 256), BF16),
            pltpu.VMEM((256, 256), BF16),
            pltpu.VMEM((128, 256), F32),
            pltpu.VMEM((128, 256), BF16),
            pltpu.VMEM((128, 256), BF16),
            pltpu.VMEM((ITERS, 8, 256), F32),
            pltpu.VMEM((2 * ITERS, 8, 128), F32),
            pltpu.VMEM((ITERS, groups, 128), F32),
            pltpu.VMEM((ITERS, groups, 128), F32),
            pltpu.VMEM((ITERS + 1, groups, 128), F32),
            pltpu.VMEM((ITERS + 1, groups, 128), F32),
            pltpu.VMEM((ITERS + 1, groups, 128), F32),
            pltpu.VMEM((8, 128), F32),
            pltpu.VMEM((peers, 8, 256), F32),
            pltpu.SMEM((32,), jnp.int32),
            pltpu.SMEM((16,), jnp.int32),
            pltpu.SMEM((16,), jnp.int32),
            pltpu.VMEM((ITERS, 1, 128), F32),
            pltpu.VMEM((ITERS, 1, 128), F32),
            pltpu.VMEM((ITERS, 1, 128), F32),
            pltpu.VMEM((ITERS + 2, 32, 8, 256), F32),
            pltpu.VMEM((ITERS + 2, 32, 8, 256), F32),
            pltpu.VMEM((ITERS, 32, 1, 128), F32),
            pltpu.VMEM((ITERS, 32, 1, 128), F32),
            pltpu.VMEM((ITERS, groups, 1, 128), F32),
            dma((9,)),
            dma((ITERS + 2,)),
            dma((ITERS,)),
            dma((ITERS,)),
            dma((ITERS,)),
            dma((ITERS + 2,)),
            dma((ITERS,)),
            dma((ITERS,)),
            dma((ITERS,)),
        ],
        compiler_params=pltpu.CompilerParams(
            collective_id=0, has_side_effects=True, vmem_limit_bytes=63 * 2**20
        ),
    )(
        load,
        row_scale,
        diag_blocks,
        off_blocks,
        off_pattern,
        partner,
        corner_coupling,
        corner_index,
        coarse_inverse,
    )
    return jnp.transpose(multipliers, (1, 0, 2)), jnp.transpose(residual, (1, 0, 2))


def solution(mesh):
    return jax.shard_map(
        on_device,
        mesh=mesh,
        in_specs=(
            P(None, ("group", "sub"), None),
            P(("group", "sub"), None),
            P(("group", "sub"), None, None),
            P(("group", "sub"), None, None),
            P(("group", "sub"), None),
            P(("group", "sub"), None),
            P(("group", "sub"), None),
            P("group", None),
            P("group", None),
        ),
        out_specs=(P(None, ("group", "sub"), None), P(None, ("group", "sub"), None)),
        check_vma=False,
    )
```

time: 1160 us -> 87.2 us (0.08)
  blocking collectives: 1100 us -> 0 us
  Pallas kernels: 0 us -> 83.2 us
  matrix products: 25.9 us -> 0 us
    psum x18 -> x0, blocking collectives: 1040 us -> none  [the longest x7 414 us: total(): return lax.psum(inner, 'group')]
    pallas_call x0 -> x1, Pallas kernels: none -> 83.2 us  [on_device(): pl.pallas_call(kernel, out_shape=(field, field), in_specs=[pl.BlockSpec(m...]
    all_to_all x4 -> x0, blocking collectives: 60.6 us -> none  [jump(): lax.all_to_all(outgoing, 'sub', split_axis=0, concat_axis=0, tiled=True)]
    dot_general x54 -> x0, matrix products: 25.9 us -> none  [the longest x4 7.48 us: on_device(): jnp.einsum('ikl,nil->nik', off_blocks, moved, preferred_element_type=jnp....]
  transfers between devices with their start and end apart: 1 -> 0, of which waited for: 1 -> 0; matrix products, arithmetic and copies ran while one was open for 0% -> 0% of each run, Pallas kernels for 0% -> 0%
where the time goes in v1:
time: 87.2 us; the launch traced here: 87 us
  Pallas kernels  83.2 us (95%)
  local copies, waits for them, and re-layouts  3.21 us (4%)
    pallas_call x1, Pallas kernels, on_device(): pl.pallas_call(kernel, out_shape=(field, field), in_specs=[pl.BlockSpec(m...  83.2 us
    unnamed x2, local copies, waits for them, and re-layouts  3.21 us

profile of v1, /device:TPU:1, one launch (start us, length us, event | category | flops | bytes accessed | tf_op | source)
XLA Modules:
  0.0 87.0 jit_solution(14680361821501102263)
XLA Ops:
  0.6 83.2 %shard_map.104 = (f32[16,8,256]{2,1,0:T(8,128)}, f32[16,8,256]{2,1,0:T(8,128)}) custom-call(f32[8,16,256]{2,1,0:T(8,128)} %load_hbm.1, f32[16,256]{1,0:T(8,128)} %scale_hbm.1, bf16[16,256,256]{2,1,0:T(8,128)(2,1)} %diag_hbm.1, bf16[16,256,256]{2,1,0:T(8,128)(2,1)} %off_hbm.1, s32[1,16]{1,0:T(1,128)} %pattern_hbm.1, s32[1,16]{1,0:T(1,128)} %partner_hbm.1, ...), custom_call_target="tpu_custom_call" | custom-call | tf_op jit(solution)/shard_map/pallas_call | solution.py:471
  83.8 1.6 %copy.11 = f32[8,16,256]{2,1,0:T(8,128)} copy(f32[8,16,256]{2,0,1:T(8,128)} %bitcast.3) | data formatting | bytes 262144
  85.4 1.6 %copy.12 = f32[8,16,256]{2,1,0:T(8,128)} copy(f32[8,16,256]{2,0,1:T(8,128)} %bitcast.2) | data formatting | bytes 262144

commit v2 on v1

--- a/solution.py
+++ b/solution.py
@@ -18,6 +18,14 @@
 def split(x):
     high = x.astype(BF16)
     return high, (x - high.astype(F32)).astype(BF16)
+
+
+def product(x, matrix):
+    high = x.astype(BF16)
+    low = x - high.astype(F32)
+    both = jnp.concatenate([high.astype(F32), low], axis=0).astype(BF16)
+    value = dot(both, matrix)
+    return value[: x.shape[0]] + value[x.shape[0] :], high
 
 
 def iota(shape, axis):
@@ -56,7 +64,10 @@
     lift_low,
     lift,
     onehot,
-    pick,
+    inverse_high,
+    inverse_low,
+    reply_high,
+    reply_low,
     local,
     info,
     norms,
@@ -96,8 +107,8 @@
 
     pairs = (
         (partner_hbm, partner_ref),
+        (load_hbm, load_ref),
         (pattern_hbm, pattern_ref),
-        (load_hbm, load_ref),
         (scale_hbm, scale_ref),
         (coupling_hbm, coupling_ref),
         (index_hbm, index_ref),
@@ -124,14 +135,10 @@
         )
 
     def all_offsets(body):
-        @pl.loop(0, peers - 4)
-        def _(s):
-            q = s // 4
-            far = 4 + ((q + 1) // 2) * (1 - 2 * (q % 2))
-            body(4 * far + s % 4)
-
-        @pl.loop(1, 4)
-        def _(o):
+        for far in (4, 3, 5, 2, 6, 1, 7):
+            for s in range(4):
+                body(4 * far + s)
+        for o in range(1, 4):
             body(o)
 
     def swap_field(source, number):
@@ -251,16 +258,29 @@
     def own(value):
         return to_column(value[0:1])
 
-    for copy in copies[:2]:
-        copy.wait()
+    copies[0].wait()
+    mates = [partner_ref[0, i] for i in range(blocks)]
 
     @pl.loop(1, peers)
     def _(o):
         peer = lax.rem(me + o, peers)
         found = jnp.int32(0)
         for i in range(blocks):
-            found = jnp.where(partner_ref[0, i] == peer, jnp.int32(i), found)
+            found = jnp.where(mates[i] == peer, jnp.int32(i), found)
         slot_block[o] = found
+
+    copies[1].wait()
+    for i in range(blocks):
+        field[i] = load_ref[:, i, :]
+
+    pl.semaphore_wait(barrier, peers - 1 + groups - 1)
+    swap_field(field, 0)
+    for copy in copies[2:5]:
+        copy.wait()
+    for i in range(blocks):
+        scale = scale_ref[i : i + 1, :]
+        coarse_rows[i] = coupling_ref[:, 256 * i : 256 * (i + 1)].astype(F32) * scale
+    swap_field(coarse_rows, 1)
 
     @pl.loop(0, blocks)
     def _(i):
@@ -269,17 +289,6 @@
             found = jnp.where(pattern_ref[0, j] == i, jnp.int32(j), found)
         inverse_pattern[i] = found
         block_slot[i] = lax.rem(me - partner_ref[0, i] + peers, peers)
-
-    for copy in copies[2:5]:
-        copy.wait()
-    for i in range(blocks):
-        field[i] = load_ref[:, i, :]
-        scale = scale_ref[i : i + 1, :]
-        coarse_rows[i] = coupling_ref[:, 256 * i : 256 * (i + 1)].astype(F32) * scale
-
-    pl.semaphore_wait(barrier, peers - 1 + groups - 1)
-    swap_field(field, 0)
-    swap_field(coarse_rows, 1)
 
     for j in range(corners):
         for i in range(blocks):
@@ -290,15 +299,22 @@
     natural = (index_ref[...] == iota((128, 256), 0)).astype(BF16)
     p = iota((256, 256), 0)
     q = iota((256, 256), 1)
-    order = ((p // 8 == (me - q % 32 + 32) % 32) & (p % 8 == q // 32)).astype(F32).astype(BF16)
-    onehot[...] = dot(natural, order).astype(BF16)
+    order = ((q // 8 == (me - p % 32 + 32) % 32) & (q % 8 == p // 32)).astype(F32).astype(BF16)
+    place = lax.dot_general(order, natural, (((1,), (1,)), ((), ())), preferred_element_type=F32)
+    onehot[...] = place.astype(BF16)
     mate = iota((1, 256), 1)
     owner = jnp.zeros((1, 256), jnp.int32) + me
     for i in range(blocks):
         owner = jnp.where((mate // 16 == i) & (mate % 16 >= 8), partner_ref[0, i], owner)
     sign = jnp.where(q % 16 >= 8, -1.0, 1.0)
     choose = jnp.where((p // 8 == owner) & (p % 8 == q % 8), sign, 0.0).astype(BF16)
-    pick[...] = dot(natural, choose).astype(BF16)
+    pick = dot(natural, choose).astype(BF16)
+    high, low = split(inverse_ref[...].T)
+    inverse_high[...] = high
+    inverse_low[...] = low
+    for part, ref in ((high, reply_high), (low, reply_low)):
+        picked = dot(part, pick).astype(BF16)
+        ref[...] = dot(onehot[...], picked).astype(BF16)
     for ref in (local, norms, ritzes, direction, residual, multipliers):
         ref[...] = jnp.zeros_like(ref)
     direction[0] = jnp.ones_like(direction[0])
@@ -343,14 +359,14 @@
                 preferred_element_type=F32,
             )
             image[i] = ahead[:8] + ahead[8:]
-        product = jnp.zeros((8, 256), F32)
+        inner = jnp.zeros((8, 256), F32)
         for i in range(blocks):
             scale = scale_ref[i : i + 1, :]
             scaled = field[i]
             total = scaled + image[i] + back[inverse_pattern[i]]
-            product = product + scale * basis[step, i] * total
+            inner = inner + scale * basis[step, i] * total
             image[i] = scale * total
-        row = to_row([jnp.sum(product, axis=1, keepdims=True)])
+        row = to_row([jnp.sum(inner, axis=1, keepdims=True)])
         swap_row(row, dot_send, dot_recv, step, dot_send_sem, dot_sem)
         swap_field(image, step + 2)
 
@@ -376,31 +392,34 @@
                 row = jnp.where(lane // 8 == k, value, row)
             swap_group(row[:1], before)
 
-        high, low = split(
-            jnp.concatenate(
-                [rows] + [pltpu.roll(rows, 128 - 8 * j, 1) for j in range(1, corners)], axis=0
-            )
-        )
-        gathered = dot(onehot[...], high) + dot(onehot[...], low)
-        high, low = split(gathered)
-        inverse_high, inverse_low = split(inverse_ref[...])
-        solved = dot(inverse_high, high) + (dot(inverse_high, low) + dot(inverse_low, high))
-        energy = jnp.sum(gathered * solved, axis=0, keepdims=True)
-        high, low = split(solved.T[:8])
-        both = jnp.concatenate([high.astype(F32), low.astype(F32)], axis=0).astype(BF16)
-        both = dot(both, pick[...])
-        local[step] = both[:8] + both[8:]
-
-        wait_row(dot_recv, step, dot_send_sem, dot_sem)
-        rows = dot_recv[step].reshape(peers, 128)
-        ritz = over(2.0 * wide(jnp.sum(rows, axis=0, keepdims=True) + energy), norm, 0.0)
+        turned = jnp.concatenate([rows, jnp.zeros((128 - 32, 128), F32)], axis=0).T
+        sides = []
+        for half in range(2):
+            side = turned[32 * half : 32 * half + 8]
+            for k in range(1, 4):
+                piece = turned[32 * half + 8 * k : 32 * half + 8 * (k + 1)]
+                side = side + pltpu.roll(piece, 32 * k, 1)
+            sides.append(side)
+        partials = jnp.concatenate(sides, axis=1)
+        value, high = product(partials, reply_high[...])
+        local[step] = value + dot(high, reply_low[...])
+        gathered, _ = product(partials, onehot[...])
+        solved, high = product(gathered, inverse_high[...])
+        solved = solved + dot(high, inverse_low[...])
+        energy = to_row([jnp.sum(gathered * solved, axis=1, keepdims=True)])
         old = over(norm * positive(info[4 + before]), info[before], 0.0)
         old = jnp.where(step > 0, old, 0.0)
-        info[4 + step] = ritz
+
+        def ritz_value():
+            wait_row(dot_recv, step, dot_send_sem, dot_sem)
+            rows = dot_recv[step].reshape(peers, 128)
+            ritz = over(2.0 * wide(jnp.sum(rows, axis=0, keepdims=True) + energy), norm, 0.0)
+            info[4 + step] = ritz
+            return ritz
 
         @pl.when(step == ITERS - 1)
         def _():
-            swap_group(ritz[:1], ITERS - 1)
+            swap_group(ritz_value()[:1], ITERS - 1)
 
         @pl.when(step > 0)
         def _():
@@ -428,6 +447,11 @@
         high, low = split(spread)
         lift[...] = dot(high, lift_high[...]) + (dot(low, lift_high[...]) + dot(high, lift_low[...]))
 
+        @pl.when(step < ITERS - 1)
+        def _():
+            ritz_value()
+
+        ritz = info[4 + step]
         shrink = to_column(1.0 / positive(ritz))
         ritz = to_column(ritz)
         old = to_column(old)
@@ -450,6 +474,12 @@
         for j in range(1, ITERS + 1):
             value = value + shares[j] * vectors[j]
         res_ref[i] = value
+
+
+def turn(a_ref, b_ref, c_ref, d_ref):
+    for i in range(a_ref.shape[0]):
+        c_ref[:, i, :] = a_ref[i]
+        d_ref[:, i, :] = b_ref[i]
 
 
 def on_device(
@@ -493,8 +523,11 @@
             pltpu.VMEM((256, 256), BF16),
             pltpu.VMEM((256, 256), BF16),
             pltpu.VMEM((128, 256), F32),
-            pltpu.VMEM((128, 256), BF16),
-            pltpu.VMEM((128, 256), BF16),
+            pltpu.VMEM((256, 128), BF16),
+            pltpu.VMEM((128, 128), BF16),
+            pltpu.VMEM((128, 128), BF16),
+            pltpu.VMEM((256, 256), BF16),
+            pltpu.VMEM((256, 256), BF16),
             pltpu.VMEM((ITERS, 8, 256), F32),
             pltpu.VMEM((2 * ITERS, 8, 128), F32),
             pltpu.VMEM((ITERS, groups, 128), F32),
@@ -539,7 +572,13 @@
         corner_index,
         coarse_inverse,
     )
-    return jnp.transpose(multipliers, (1, 0, 2)), jnp.transpose(residual, (1, 0, 2))
+    turned = jax.ShapeDtypeStruct(load.shape, F32)
+    return pl.pallas_call(
+        turn,
+        out_shape=(turned, turned),
+        in_specs=[vmem, vmem],
+        out_specs=(vmem, vmem),
+    )(multipliers, residual)
 
 
 def solution(mesh):

time: 87.2 us -> 84.3 us (0.967)
  local copies, waits for them, and re-layouts: 3.21 us -> 0 us
    unnamed x2 -> x0, local copies, waits for them, and re-layouts: 3.21 us -> none
    pallas_call x0 -> x1, Pallas kernels: none -> 1.77 us  [on_device(): pl.pallas_call(turn, out_shape=(turned, turned), in_specs=[vmem, vmem], o...]
    pallas_call x1, Pallas kernels: 83.2 us -> 81.7 us  [on_device(): pl.pallas_call(kernel, out_shape=(field, field), in_specs=[pl.BlockSpec(m...]
where the time goes in v2:
time: 84.3 us; the launch traced here: 84.2 us
  Pallas kernels  83.5 us (99%)
    pallas_call x1, Pallas kernels, on_device(): pl.pallas_call(kernel, out_shape=(field, field), in_specs=[pl.BlockSpec(m...  81.7 us
    pallas_call x1, Pallas kernels, on_device(): pl.pallas_call(turn, out_shape=(turned, turned), in_specs=[vmem, vmem], o...  1.77 us

profile of v2, /device:TPU:1, one launch (start us, length us, event | category | flops | bytes accessed | tf_op | source)
XLA Modules:
  0.0 84.2 jit_solution(996594227709996572)
XLA Ops:
  0.6 81.7 %shard_map.104 = (f32[16,8,256]{2,1,0:T(8,128)}, f32[16,8,256]{2,1,0:T(8,128)}) custom-call(f32[8,16,256]{2,1,0:T(8,128)} %load_hbm.1, f32[16,256]{1,0:T(8,128)} %scale_hbm.1, bf16[16,256,256]{2,1,0:T(8,128)(2,1)} %diag_hbm.1, bf16[16,256,256]{2,1,0:T(8,128)(2,1)} %off_hbm.1, s32[1,16]{1,0:T(1,128)} %pattern_hbm.1, s32[1,16]{1,0:T(1,128)} %partner_hbm.1, ...), custom_call_target="tpu_custom_call" | custom-call | tf_op jit(solution)/shard_map/pallas_call | solution.py:501
  82.4 1.8 %shard_map.105 = (f32[8,16,256]{2,1,0:T(8,128)}, f32[8,16,256]{2,1,0:T(8,128)}) custom-call(f32[16,8,256]{2,1,0:T(8,128)} %get-tuple-element.4.a_ref, f32[16,8,256]{2,1,0:T(8,128)} %get-tuple-element.5.b_ref), custom_call_target="tpu_custom_call" | custom-call | tf_op jit(solution)/shard_map/pallas_call | solution.py:576
